TPU v7x, 256 devices: a whole 4x4x8 slice. The times are simulated.
256 devices in a mesh: mp: 4 (over y), nodes: 64 (over z, x, core).
Axes of the slice: x: 4, y: 4, z: 8, core: 2. Of those that a mesh axis runs over, the one named last changes fastest.
Arguments:
- grid_latent: float32 [131072, 512], P('nodes'), may hold values from -6 to 6
- mesh_latent: float32 [8192, 512], P('nodes'), may hold values from -250 to 250
- enc_grid_w: float32 [512, 512], P(None, 'mp'), may hold values from -0.25 to 0.25
- enc_mesh_w: float32 [512, 512], P(None, 'mp'), may hold values from -0.25 to 0.25
- enc_out_w: float32 [512, 512], P('mp'), may hold values from -0.25 to 0.25
- block_gain: float32 [512], replicated, may hold values from 0.5 to 1.5
- query_w: float32 [512, 512], P(None, 'mp'), may hold values from -1 to 1
- key_w: float32 [512, 512], P(None, 'mp'), may hold values from -1 to 1
- value_w: float32 [512, 512], P(None, 'mp'), may hold values from -0.25 to 0.25
- out_w: float32 [512, 512], P('mp'), may hold values from -0.25 to 0.25
- up_w: float32 [512, 2048], P(None, 'mp'), may hold values from -0.25 to 0.25
- down_w: float32 [2048, 512], P('mp'), may hold values from -0.125 to 0.125
- dec_gain: float32 [512], replicated, may hold values from 0.5 to 1.5
- dec_grid_w: float32 [512, 512], P(None, 'mp'), may hold values from -0.25 to 0.25
- dec_mesh_w: float32 [512, 512], P(None, 'mp'), may hold values from -0.25 to 0.25
- dec_out_w: float32 [512, 512], P('mp'), may hold values from -0.25 to 0.25
- neighbor_blocks: int32 [64, 16], replicated, may hold values from 0 to 63, as said below
- enc_tiles: int32 [2048, 2], P('nodes'), may hold values from -1 to 1023, as said below
- enc_edges: int32 [2048, 2, 128], P('nodes'), may hold values from 0 to 127
- dec_tiles: int32 [3072, 2], P('nodes'), may hold values from 0 to 1023, as said below
- dec_edges: int32 [3072, 2, 128], P('nodes'), may hold values from 0 to 127
Outputs:
- grid_out: float32 [131072, 512], P('nodes', 'mp')
Inputs may be any that keep to these rules, and one draw needn't show every extreme that they name: `neighbor_blocks`: rows i * 1 to (i + 1) - 1 are the query blocks of index i of nodes; among all entries of those rows, the blocks of any one index j of nodes (ids j * 1 to (j + 1) - 1) are named at most 1 times, and for every i some j is named exactly 1 times. Entries may repeat. `enc_tiles`: tile slots i * 32 to (i + 1) * 32 - 1 belong to index i of nodes; a live tile names a grid block and a mesh block both of index i; an unused slot holds -1 in both columns; on each index the live slots come first, their number differs between indices, and some index has all 32 slots live. `dec_tiles`: tiles i * 48 to (i + 1) * 48 - 1 belong to index i of nodes; each names a grid block of index i and a mesh block of index i - 1, i or i + 1 of nodes (counted around the axis).
All inputs are finite; a program needn't handle non-finite values.
Results may differ from a plain program's by a relative error of at most 0.000098.
Values sent between devices are 32-bit elements; how exact they have to be, the bound alone decides.
A program may use at most 128 MiB of HBM per device.

v0:
```python
import math
import jax
import jax.numpy as jnp
from jax import lax
from jax.sharding import PartitionSpec as P

HEAD_DIM = 128
NODE_BLOCK = 128
FULL_PRECISION = lax.Precision.HIGHEST


def copy_for_each(shard, axis):
    devices = lax.axis_size(axis)
    return lax.all_to_all(
        jnp.broadcast_to(shard[None], (devices, *shard.shape)), axis, 0, 0, tiled=True
    )


def taken_together(shard, axis):
    everything = copy_for_each(shard, axis)
    return jnp.sum(everything, axis=0)


def padded(shard, sides, width):
    for axis, dim in sides:
        devices, length = (lax.axis_size(axis), shard.shape[dim])
        up = [(i, (i + 1) % devices) for i in range(devices)]
        down = [(j, i) for i, j in up]
        last = lax.slice_in_dim(shard, length - width, length, axis=dim)
        initial = lax.slice_in_dim(shard, 0, width, axis=dim)
        before = lax.ppermute(last, axis, up)
        after = lax.ppermute(initial, axis, down)
        shard = jnp.concatenate([before, shard, after], axis=dim)
    return shard


def product(matrix, weight):
    return jnp.dot(matrix, weight, precision=FULL_PRECISION, preferred_element_type=jnp.float32)


def layer_norm(inputs, scales):
    centre = jnp.mean(inputs, axis=-1, keepdims=True)
    shifted = inputs - centre
    spread = jnp.mean(shifted * shifted, axis=-1, keepdims=True)
    return shifted * lax.rsqrt(spread + 1e-05) * scales


def edge_pass(
    source_side, target_side, source_block, target_block, edge_ids, tile_live, target_blocks
):
    source = source_block[:, None] * NODE_BLOCK + edge_ids[:, 0, :]
    target = target_block[:, None] * NODE_BLOCK + edge_ids[:, 1, :]
    message = jax.nn.silu(source_side[source] + target_side[target]) * tile_live[:, None, None]
    within = (edge_ids[:, 1, :][:, None, :] == jnp.arange(NODE_BLOCK)[None, :, None]).astype(
        jnp.float32
    )
    tile_sums = jnp.einsum("tne,teh->tnh", within, message, precision=FULL_PRECISION)
    placing = (target_block[None, :] == jnp.arange(target_blocks)[:, None]).astype(jnp.float32)
    summed = jnp.einsum("bt,tnh->bnh", placing, tile_sums, precision=FULL_PRECISION)
    return summed.reshape(target_blocks * NODE_BLOCK, -1)


def per_device(
    grid_latent,
    mesh_latent,
    enc_grid_w,
    enc_mesh_w,
    enc_out_w,
    block_gain,
    query_w,
    key_w,
    value_w,
    out_w,
    up_w,
    down_w,
    dec_gain,
    dec_grid_w,
    dec_mesh_w,
    dec_out_w,
    neighbor_blocks,
    enc_tiles,
    enc_edges,
    dec_tiles,
    dec_edges,
):
    me_node = lax.axis_index("nodes")
    nodes_count = lax.axis_size("nodes")
    grid_rows = grid_latent.shape[0]
    node_rows = mesh_latent.shape[0]
    grid_blocks = grid_rows // NODE_BLOCK
    node_blocks = node_rows // NODE_BLOCK
    grid_enc = product(grid_latent, enc_grid_w)
    mesh_enc = product(mesh_latent, enc_mesh_w)
    tile_live = enc_tiles[:, 0] >= 0
    source_block = jnp.where(tile_live, enc_tiles[:, 0] - me_node * grid_blocks, 0)
    target_block = jnp.where(tile_live, enc_tiles[:, 1] - me_node * node_blocks, 0)
    enc_agg = edge_pass(
        grid_enc,
        mesh_enc,
        source_block,
        target_block,
        enc_edges,
        tile_live.astype(jnp.float32),
        node_blocks,
    )
    enc_total = taken_together(product(enc_agg, enc_out_w), "mp")
    mesh_one = mesh_latent + enc_total
    normed = layer_norm(mesh_one, block_gain)
    queries = product(normed, query_w)
    key_rows = product(normed, key_w)
    value_rows = product(normed, value_w)
    head_cols = queries.shape[1]
    heads_here = head_cols // HEAD_DIM
    key_values = jnp.concatenate([key_rows, value_rows], axis=1)
    query_blocks = queries.reshape(node_blocks, NODE_BLOCK, heads_here, HEAD_DIM)
    own_lists = lax.dynamic_slice_in_dim(neighbor_blocks, me_node * node_blocks, node_blocks, 0)
    key_piece = lax.all_gather(key_values, "nodes", axis=0, tiled=True)
    running_max = jnp.full((node_blocks, heads_here, NODE_BLOCK), -1e30, jnp.float32)
    row_count = key_piece.shape[0]
    piece_block = jnp.arange(row_count) // NODE_BLOCK
    repeats = jnp.sum(
        (own_lists[:, :, None] == piece_block[None, None, :]).astype(jnp.float32), axis=1
    )
    near_keys = key_piece[:, :head_cols].reshape(row_count, heads_here, HEAD_DIM)
    near_values = key_piece[:, head_cols:].reshape(row_count, heads_here, HEAD_DIM)
    scores = jnp.einsum(
        "bqhd,khd->bhqk", query_blocks, near_keys, precision=FULL_PRECISION
    ) / math.sqrt(HEAD_DIM)
    scores = jnp.where((repeats > 0)[:, None, None, :], scores, -1e30)
    new_max = jnp.maximum(running_max, jnp.max(scores, axis=-1))
    weights = jnp.exp(scores - new_max[..., None]) * repeats[:, None, None, :]
    running_sum = jnp.sum(weights, axis=-1)
    running_out = jnp.einsum("bhqk,khd->bhqd", weights, near_values, precision=FULL_PRECISION)
    running_max, running_sum, running_out = (new_max, running_sum, running_out)
    attended = (
        (running_out / running_sum[..., None]).transpose(0, 2, 1, 3).reshape(node_rows, head_cols)
    )
    hidden = jax.nn.silu(product(normed, up_w))
    block_total = taken_together(product(attended, out_w) + product(hidden, down_w), "mp")
    mesh_two = mesh_one + block_total
    mesh_normed = layer_norm(mesh_two, dec_gain)
    all_blocks = node_blocks * nodes_count
    dec_source = (dec_tiles[:, 0] - (me_node - 1) * node_blocks) % all_blocks
    dec_target = dec_tiles[:, 1] - me_node * grid_blocks
    mesh_dec = product(mesh_normed, dec_mesh_w)
    grid_dec = product(grid_latent, dec_grid_w)
    beside_all = padded(mesh_dec, (("nodes", 0),), node_rows)
    every_tile = jnp.ones((dec_tiles.shape[0],), jnp.float32)
    dec_agg = edge_pass(
        beside_all, grid_dec, dec_source, dec_target, dec_edges, every_tile, grid_blocks
    )
    decoded = lax.psum_scatter(product(dec_agg, dec_out_w), "mp", scatter_dimension=1, tiled=True)
    share_cols = decoded.shape[1]
    grid_share = lax.dynamic_slice_in_dim(
        grid_latent, lax.axis_index("mp") * share_cols, share_cols, 1
    )
    return grid_share + decoded


def solution(mesh):
    in_specs = (
        P("nodes", None),
        P("nodes", None),
        P(None, "mp"),
        P(None, "mp"),
        P("mp", None),
        P(),
        P(None, "mp"),
        P(None, "mp"),
        P(None, "mp"),
        P("mp", None),
        P(None, "mp"),
        P("mp", None),
        P(),
        P(None, "mp"),
        P(None, "mp"),
        P("mp", None),
        P(),
        P("nodes", None),
        P("nodes", None, None),
        P("nodes", None),
        P("nodes", None, None),
    )
    out_specs = P("nodes", "mp")
    return jax.shard_map(
        per_device, mesh=mesh, in_specs=in_specs, out_specs=out_specs, check_vma=False
    )
```

profile of v0, /device:TPU:1, one launch (start us, length us, event | category | flops | bytes accessed | tf_op | source)
XLA Modules:
  0.0 320.2 jit_solution(5665436345619726725)
XLA Ops:
  8.1 0.9 fusion.91
  8.9 5.2 %fusion.94 = f32[2048,128]{1,0:T(8,128)S(1)} fusion(f32[2048,512]{1,0:T(8,128)} %param.21, f32[512,128]{1,0:T(8,128)} %param.23), kind=kOutput, calls=%fused_computation.123 | convolution fusion | flops 1610612736 | bytes 5505024 | tf_op jit(solution)/shard_map/dot_general | solution.py:38
  14.3 14.1 %gather_fusion = f32[4096,128]{1,0:T(8,128)} fusion(f32[2048,128]{1,0:T(8,128)S(1)} %fusion.94, s32[4096]{0:T(1024)S(1)} %get-tuple-element.20), kind=kCustom, calls=%fused_computation | custom fusion | bytes 4210688 | tf_op jit(solution)/shard_map/gather | solution.py:53
  28.8 14.1 %gather_fusion.1 = f32[4096,128]{1,0:T(8,128)} fusion(f32[128,128]{1,0:T(8,128)S(1)} %fusion.95, s32[4096]{0:T(1024)S(1)} %get-tuple-element.21), kind=kCustom, calls=%fused_computation.1 | custom fusion | bytes 4210688 | tf_op jit(solution)/shard_map/gather | solution.py:53
  42.9 1.8 add.221
  44.7 1.9 fusion.19
  46.6 2.0 fusion.15
  49.1 19.0 %all_to_all.10 = f32[4,128,512]{2,1,0:T(8,128)S(1)} all-to-all(f32[4,128,512]{2,1,0:T(8,128)S(1)} %broadcast_in_dim.17), channel_id=1, replica_groups=mesh['mp'=4,'nodes'=64] {'mp'}, dimensions={0} | all-to-all | bytes 2097152 | tf_op jit(solution)/shard_map/all_to_all | solution.py:14
  68.2 1.1 fusion.89
  69.6 1.6 fusion.87
  71.2 1.6 fusion.86
  73.9 1.4 fusion.85
  76.8 84.9 %all-gather.2.cloned.1.call-done = f32[8192,256]{0,1:T(8,128)} async-done(((f32[128,256]{0,1:T(8,128)}), f32[8192,256]{0,1:T(8,128)}) %all-gather.2.cloned.1.call-update) | async-done | bytes 8388624 | tf_op jit(solution)/shard_map/all_gather | solution.py:117
  161.6 10.2 %fusion.92 = (f32[128]{0:T(128)S(1)}, f32[1,8192,1,128]{3,1,2,0:T(8,128)S(1)}) fusion(f32[128,128]{1,0:T(8,128)S(1)} %fusion.85, f32[8192,256]{0,1:T(8,128)} %all-gather.2.cloned.1.call-done, pred[8192]{0:T(1024)(128)(4,1)S(1)} %broadcast_compare_fusion), kind=kOutput, calls=%fused_computation.121 | convolution fusion | flops 1613758336 | bytes 8462848 | tf_op jit(solution)/shard_map/bqhd,khd->bhqk/dot_general | solution.py:126
  171.8 3.5 %fusion.6 = f32[128]{0:T(128)S(1)} fusion(f32[1,8192,1,128]{3,1,2,0:T(8,128)S(1)} %get-tuple-element.19, f32[8192]{0:T(1024)S(1)} %convert_reduce_fusion, f32[128]{0:T(128)S(1)} %broadcast_maximum_fusion), kind=kLoop, calls=%fused_computation.12 | loop fusion | flops 3145600 | bytes 4228096 | tf_op jit(solution)/shard_map/reduce_sum | solution.py:132
  175.3 5.0 %fusion.38 = f32[128,128]{0,1:T(8,128)S(1)} fusion(f32[1,8192,1,128]{3,1,2,0:T(8,128)S(1)} %get-tuple-element.19, f32[8192]{0:T(1024)S(1)} %convert_reduce_fusion, f32[128]{0:T(128)S(1)} %broadcast_maximum_fusion, f32[8192,256]{0,1:T(8,128)S(1)} %copy-done.1, f32[128]{0:T(128)S(1)} %fusion.6), kind=kOutput, calls=%fused_computation.39 | convolution fusion | flops 1612726272 | bytes 8487936 | tf_op jit(solution)/shard_map/bhqk,khd->bhqd/dot_general | solution.py:133
  180.8 1.1 broadcast_in_dim.21
  181.9 4.0 %all-to-all-start.1 = ((f32[4,128,512]{2,1,0:T(8,128)}), f32[4,128,512]{2,1,0:T(8,128)S(1)}, u32[]{:S(2)}, u32[]{:S(2)}) async-start(f32[4,128,512]{2,1,0:T(8,128)} %broadcast_in_dim.21), calls=%async_computation.1 | async-start | bytes 2097152 | tf_op jit(solution)/shard_map/all_to_all | solution.py:14
  186.0 5.2 %fusion.97 = f32[2048,128]{1,0:T(8,128)S(1)} fusion(f32[2048,512]{1,0:T(8,128)} %param.21, f32[512,128]{1,0:T(8,128)} %param.34), kind=kOutput, calls=%fused_computation.126 | convolution fusion | flops 1610612736 | bytes 5505024 | tf_op jit(solution)/shard_map/dot_general | solution.py:38
  191.2 9.3 %all-to-all-done.1 = f32[4,128,512]{2,1,0:T(8,128)S(1)} async-done(((f32[4,128,512]{2,1,0:T(8,128)}), f32[4,128,512]{2,1,0:T(8,128)S(1)}, u32[]{:S(2)}, u32[]{:S(2)}) %all-to-all-start.1) | async-done | bytes 1048608 | tf_op jit(solution)/shard_map/all_to_all | solution.py:14
  200.6 0.8 reduce_sum.77
  201.4 1.1 fusion.88
  202.6 1.4 fusion.46
  204.0 3.1 collective-permute-start
  207.2 20.9 %gather_fusion.3 = f32[6144,128]{1,0:T(8,128)} fusion(f32[2048,128]{1,0:T(8,128)S(1)} %fusion.97, s32[6144]{0:T(1024)S(1)} %get-tuple-element.23), kind=kCustom, calls=%fused_computation.3 | custom fusion | bytes 6316032 | tf_op jit(solution)/shard_map/gather | solution.py:53
  228.1 20.9 %gather_fusion.2 = f32[6144,128]{1,0:T(8,128)} fusion(f32[384,128]{1,0:T(8,128)S(1)} %pad_maximum_fusion, s32[6144]{0:T(1024)S(1)} %get-tuple-element.22), kind=kCustom, calls=%fused_computation.2 | custom fusion | bytes 6316032 | tf_op jit(solution)/shard_map/gather | solution.py:53
  249.1 3.2 add.222
  252.2 2.9 fusion.9
  255.2 2.9 fusion.7
  258.5 4.9 %fusion.98 = f32[2048,512]{1,0:T(8,128)} fusion(f32[2048,128]{1,0:T(8,128)S(1)} %bitcast.97, f32[128,512]{1,0:T(8,128)S(1)} %copy-done.8), kind=kOutput, calls=%fused_computation.127 | convolution fusion | flops 1610612736 | bytes 5505024 | tf_op jit(solution)/shard_map/dot_general | solution.py:38
  263.4 47.3 %reduce-scatter.2.cloned.1.call-done = f32[2048,128]{1,0:T(8,128)} async-done(((f32[2048,512]{1,0:T(8,128)}), f32[2048,128]{1,0:T(8,128)}) %reduce-scatter.2.cloned.1.call-update) | async-done | bytes 1048592 | tf_op jit(solution)/shard_map/reduce_scatter | solution.py:152
  310.7 2.6 dynamic-slice_add_fusion
  (64 shorter events, 6.5 us)
Async XLA Ops:
  6.5 68.7 %copy-start = (f32[512,512]{1,0:T(8,128)S(1)}, f32[512,512]{1,0:T(8,128)}, u32[]{:S(2)}) copy-start(f32[512,512]{1,0:T(8,128)} %param.31) | copy-start | bytes 3145732
  6.5 155.1 %all-gather.2.cloned.1.call-start = ((), (), s32[]{:S(2)}) async-start(), calls=%async_computation.3 | async-start | bytes 8519680 | tf_op jit(solution)/shard_map/all_gather | solution.py:117
  14.2 14.1 %copy-start.4 = (f32[128,512]{1,0:T(8,128)S(1)}, f32[128,512]{1,0:T(8,128)}, u32[]{:S(2)}) copy-start(f32[128,512]{1,0:T(8,128)} %param.22) | copy-start | bytes 786436
  14.3 14.1 %copy-start.5 = (f32[512,128]{1,0:T(8,128)S(1)}, f32[512,128]{1,0:T(8,128)}, u32[]{:S(2)}) copy-start(f32[512,128]{1,0:T(8,128)} %param.24) | copy-start | bytes 786436
  28.8 14.1 %copy-start.2 = (f32[4096,128]{1,0:T(8,128)S(1)}, f32[4096,128]{1,0:T(8,128)}, u32[]{:S(2)}) copy-start(f32[4096,128]{1,0:T(8,128)} %gather_fusion) | copy-start | bytes 6291460
  44.7 1.9 copy-start.12
  44.7 3.9 %copy-start.6 = (f32[128,512]{1,0:T(8,128)S(1)}, f32[128,512]{1,0:T(8,128)}, u32[]{:S(2)}) copy-start(f32[128,512]{1,0:T(8,128)} %param.25) | copy-start | bytes 786436
  48.6 21.0 %copy-start.10 = (f32[512]{0:T(512)S(1)}, f32[512]{0:T(512)}, u32[]{:S(2)}) copy-start(f32[512]{0:T(512)} %param.26) | copy-start | bytes 6148
  49.1 24.4 %copy-start.11 = (s32[64,16]{0,1:T(8,128)S(1)}, s32[64,16]{0,1:T(8,128)}, u32[]{:S(2)}) copy-start(s32[64,16]{0,1:T(8,128)} %param.37) | copy-start | bytes 12292
  68.1 7.9 %copy-start.3 = (f32[512,512]{1,0:T(8,128)S(1)}, f32[512,512]{1,0:T(8,128)}, u32[]{:S(2)}) copy-start(f32[512,512]{1,0:T(8,128)} %param.32) | copy-start | bytes 3145732
  161.6 13.7 %copy-start.1 = (f32[8192,256]{0,1:T(8,128)S(1)}, f32[8192,256]{0,1:T(8,128)}, u32[]{:S(2)}) copy-start(f32[8192,256]{0,1:T(8,128)} %all-gather.2.cloned.1.call-done) | copy-start | bytes 25165828
  175.3 5.0 %copy-start.7 = (f32[128,512]{1,0:T(8,128)S(1)}, f32[128,512]{1,0:T(8,128)}, u32[]{:S(2)}) copy-start(f32[128,512]{1,0:T(8,128)} %param.30) | copy-start | bytes 786436
  180.3 5.6 %copy-start.14 = (s32[48,2]{0,1:T(2,128)S(1)}, s32[48,2]{0,1:T(2,128)}, u32[]{:S(2)}) copy-start(s32[48,2]{0,1:T(2,128)} %param.40) | copy-start | bytes 1156
  180.4 5.6 %copy-start.9 = (s32[48,2,128]{2,1,0:T(2,128)S(1)}, s32[48,2,128]{2,1,0:T(2,128)}, u32[]{:S(2)}) copy-start(s32[48,2,128]{2,1,0:T(2,128)} %param.41) | copy-start | bytes 147460
  181.9 18.7 %all-to-all-start.1 = ((f32[4,128,512]{2,1,0:T(8,128)}), f32[4,128,512]{2,1,0:T(8,128)S(1)}, u32[]{:S(2)}, u32[]{:S(2)}) async-start(f32[4,128,512]{2,1,0:T(8,128)} %broadcast_in_dim.21), calls=%async_computation.1 | async-start | bytes 2097152 | tf_op jit(solution)/shard_map/all_to_all | solution.py:14
  185.9 124.8 %reduce-scatter.2.cloned.1.call-start = ((), (), s32[]{:S(2)}) async-start(), calls=%async_computation.4 | async-start | bytes 5242880 | tf_op jit(solution)/shard_map/reduce_scatter | solution.py:152
  186.0 16.6 %copy-start.13 = (f32[512]{0:T(512)S(1)}, f32[512]{0:T(512)}, u32[]{:S(2)}) copy-start(f32[512]{0:T(512)} %param.33) | copy-start | bytes 6148
  204.0 24.1 %collective-permute-start = (f32[128,128]{1,0:T(8,128)S(1)}, f32[128,128]{1,0:T(8,128)S(1)}, u32[]{:S(2)}, u32[]{:S(2)}) collective-permute-start(f32[128,128]{1,0:T(8,128)S(1)} %fusion.46), channel_id=1, source_target_pairs={{0,1},{1,2},{2,3},{3,4},{4,5},{5,6},{6,7},{7,8},{8,9},{9,10},{10,1... | collective-permute-start | bytes 196616 | tf_op jit(solution)/shard_map/ppermute | solution.py:31
  207.1 21.0 %collective-permute-start.1 = (f32[128,128]{1,0:T(8,128)S(1)}, f32[128,128]{1,0:T(8,128)S(1)}, u32[]{:S(2)}, u32[]{:S(2)}) collective-permute-start(f32[128,128]{1,0:T(8,128)S(1)} %fusion.46), channel_id=1, source_target_pairs={{1,0},{2,1},{3,2},{4,3},{5,4},{6,5},{7,6},{8,7},{9,8},{10,9},{11,1... | collective-permute-start | bytes 196616 | tf_op jit(solution)/shard_map/ppermute | solution.py:32
  255.2 3.3 %copy-start.8 = (f32[128,512]{1,0:T(8,128)S(1)}, f32[128,512]{1,0:T(8,128)}, u32[]{:S(2)}) copy-start(f32[128,512]{1,0:T(8,128)} %param.36) | copy-start | bytes 786436
Sparse Core Ops, SparseCore 0:
  73.6 87.9 all-gather.1
  263.6 47.1 reduce-scatter.1
where the time goes:
time: 321 us; the launch traced here: 320 us
  waiting for transfers between devices  142 us (44%)
  local copies, waits for them, and re-layouts  72.8 us (23%)
  matrix products  48.9 us (15%)
  blocking collectives  19 us (6%)
  other arithmetic  17.1 us (5%)
  between operations  13.8 us (4%)
  starting transfers between devices  7.08 us (2%)
    all_gather x1, waiting for transfers between devices, per_device(): key_piece = lax.all_gather(key_values, 'nodes', axis=0, tiled=True)  84.9 us
    reduce_scatter x1, waiting for transfers between devices, per_device(): lax.psum_scatter(product(dec_agg, dec_out_w), 'mp', scatter_dimension=1,...  47.3 us
    gather x2, local copies, waits for them, and re-layouts, edge_pass(): source_side[source] + target_side[target]  35 us
    gather x2, local copies, waits for them, and re-layouts, edge_pass(): target_side[target]  35 us
    dot_general x12, matrix products, product(): jnp.dot(matrix, weight, precision=FULL_PRECISION, preferred_element_type=...  24 us
    all_to_all x1, blocking collectives, copy_for_each(): lax.all_to_all(jnp.broadcast_to(shard[None], (devices, *shard.shape)), ax...  19 us
    dot_general x1, matrix products, per_device(): jnp.einsum('bqhd,khd->bhqk', query_blocks, near_keys, precision=FULL_PREC...  10.2 us
    all_to_all x1, waiting for transfers between devices, copy_for_each(): lax.all_to_all(jnp.broadcast_to(shard[None], (devices, *shard.shape)), ax...  9.34 us
  transfers between devices with their start and end apart: 5, of which 3 were waited for; matrix products, arithmetic and copies ran while one was open for 9% of the time, Pallas kernels for 0%

commit v1 on v0

--- a/solution.py
+++ b/solution.py
@@ -114,7 +114,8 @@
     key_values = jnp.concatenate([key_rows, value_rows], axis=1)
     query_blocks = queries.reshape(node_blocks, NODE_BLOCK, heads_here, HEAD_DIM)
     own_lists = lax.dynamic_slice_in_dim(neighbor_blocks, me_node * node_blocks, node_blocks, 0)
-    key_piece = lax.all_gather(key_values, "nodes", axis=0, tiled=True)
+    copies = jnp.concatenate([key_values] * lax.axis_size("nodes"), axis=0)
+    key_piece = lax.all_to_all(copies, "nodes", 0, 0, tiled=True)
     running_max = jnp.full((node_blocks, heads_here, NODE_BLOCK), -1e30, jnp.float32)
     row_count = key_piece.shape[0]
     piece_block = jnp.arange(row_count) // NODE_BLOCK

time: 321 us -> 459 us (1.43); the launches traced: 320 us -> 450 us
  waiting for transfers between devices: 142 us -> 232 us
  starting transfers between devices: 7.08 us -> 37 us
  local copies, waits for them, and re-layouts: 72.8 us -> 86.6 us
    all_to_all x0 -> x1, waiting for transfers between devices: none -> 180 us  [per_device(): key_piece = lax.all_to_all(copies, 'nodes', 0, 0, tiled=True)]
    all_gather x1 -> x0, waiting for transfers between devices: 84.9 us -> none  [per_device(): key_piece = lax.all_gather(key_values, 'nodes', axis=0, tiled=True)]
    all_to_all x0 -> x1, starting transfers between devices: none -> 25.2 us  [per_device(): key_piece = lax.all_to_all(copies, 'nodes', 0, 0, tiled=True)]
    all_to_all x0 -> x2, local copies, waits for them, and re-layouts: none -> 13.3 us  [per_device(): key_piece = lax.all_to_all(copies, 'nodes', 0, 0, tiled=True)]
    ppermute x1, starting transfers between devices: 3.07 us -> 8.23 us  [padded(): before = lax.ppermute(last, axis, up)]
  transfers between devices with their start and end apart: 5 -> 5, of which waited for: 3 -> 3; matrix products, arithmetic and copies ran while one was open for 9% -> 6% of each run, Pallas kernels for 0% -> 0%
where the time goes in v1:
time: 459 us; the launch traced here: 450 us
  waiting for transfers between devices  232 us (51%)
  local copies, waits for them, and re-layouts  86.6 us (19%)
  matrix products  45.7 us (10%)
  starting transfers between devices  37 us (8%)
  blocking collectives  19 us (4%)
  between operations  14.8 us (3%)
  other arithmetic  14.6 us (3%)
    all_to_all x1, waiting for transfers between devices, per_device(): key_piece = lax.all_to_all(copies, 'nodes', 0, 0, tiled=True)  180 us
    reduce_scatter x1, waiting for transfers between devices, per_device(): lax.psum_scatter(product(dec_agg, dec_out_w), 'mp', scatter_dimension=1,...  46.9 us
    gather x2, local copies, waits for them, and re-layouts, edge_pass(): source_side[source] + target_side[target]  35.3 us
    gather x2, local copies, waits for them, and re-layouts, edge_pass(): target_side[target]  35.3 us
    all_to_all x1, starting transfers between devices, per_device(): key_piece = lax.all_to_all(copies, 'nodes', 0, 0, tiled=True)  25.2 us
    dot_general x12, matrix products, product(): jnp.dot(matrix, weight, precision=FULL_PRECISION, preferred_element_type=...  20.2 us
    all_to_all x1, blocking collectives, copy_for_each(): lax.all_to_all(jnp.broadcast_to(shard[None], (devices, *shard.shape)), ax...  19 us
    all_to_all x2, local copies, waits for them, and re-layouts, per_device(): key_piece = lax.all_to_all(copies, 'nodes', 0, 0, tiled=True)  13.3 us
  transfers between devices with their start and end apart: 5, of which 3 were waited for; matrix products, arithmetic and copies ran while one was open for 6% of the time, Pallas kernels for 0%

profile of v1, /device:TPU:1, one launch (start us, length us, event | category | flops | bytes accessed | tf_op | source)
XLA Modules:
  0.0 449.8 jit_solution(13438826603909842274)
XLA Ops:
  6.5 0.8 convert_bitcast_fusion
  7.3 0.8 multiply_bitcast_fusion.1
  8.1 0.9 fusion.91
  8.9 5.2 %fusion.94 = f32[2048,128]{1,0:T(8,128)S(1)} fusion(f32[2048,512]{1,0:T(8,128)} %param.21, f32[512,128]{1,0:T(8,128)} %param.23), kind=kOutput, calls=%fused_computation.188 | convolution fusion | flops 1610612736 | bytes 5505024 | tf_op jit(solution)/shard_map/dot_general | solution.py:38
  14.3 14.2 %gather_fusion = f32[4096,128]{1,0:T(8,128)} fusion(f32[2048,128]{1,0:T(8,128)S(1)} %fusion.94, s32[4096]{0:T(1024)S(1)} %get-tuple-element.22), kind=kCustom, calls=%fused_computation | custom fusion | bytes 4210688 | tf_op jit(solution)/shard_map/gather | solution.py:53
  28.9 14.2 %gather_fusion.1 = f32[4096,128]{1,0:T(8,128)} fusion(f32[128,128]{1,0:T(8,128)S(1)} %fusion.95, s32[4096]{0:T(1024)S(1)} %get-tuple-element.23), kind=kCustom, calls=%fused_computation.1 | custom fusion | bytes 4210688 | tf_op jit(solution)/shard_map/gather | solution.py:53
  43.1 1.8 add.221
  45.0 1.9 fusion.19
  46.9 2.0 fusion.15
  49.3 19.0 %all_to_all.22 = f32[4,128,512]{2,1,0:T(8,128)S(1)} all-to-all(f32[4,128,512]{2,1,0:T(8,128)S(1)} %broadcast_in_dim.17), channel_id=1, replica_groups=mesh['mp'=4,'nodes'=64] {'mp'}, dimensions={0} | all-to-all | bytes 2097152 | tf_op jit(solution)/shard_map/all_to_all | solution.py:14
  71.3 4.3 copy_bitcast_fusion
  75.7 25.2 %all-to-all-start.1 = ((f32[64,128,256]{1,2,0:T(8,128)}), f32[64,128,256]{1,2,0:T(8,128)}, u32[]{:S(2)}, u32[]{:S(2)}) async-start(f32[64,128,256]{1,2,0:T(8,128)} %copy_bitcast_fusion), calls=%async_computation.1 | async-start | bytes 16777216 | tf_op jit(solution)/shard_map/all_to_all | solution.py:118
  101.8 0.7 fusion.84
  102.5 0.8 fusion.49
  103.3 179.9 %all-to-all-done.1 = f32[64,128,256]{1,2,0:T(8,128)} async-done(((f32[64,128,256]{1,2,0:T(8,128)}), f32[64,128,256]{1,2,0:T(8,128)}, u32[]{:S(2)}, u32[]{:S(2)}) %all-to-all-start.1) | async-done | bytes 8388640 | tf_op jit(solution)/shard_map/all_to_all | solution.py:118
  283.2 9.0 %copy.41 = f32[64,128,256]{2,1,0:T(8,128)} copy(f32[64,128,256]{1,2,0:T(8,128)} %all-to-all-done.1) | data formatting | bytes 16777216 | tf_op jit(solution)/shard_map/all_to_all | solution.py:118
  292.2 7.8 %fusion.92 = (f32[128]{0:T(128)S(1)}, f32[1,8192,1,128]{3,1,2,0:T(8,128)S(1)}) fusion(f32[128,128]{1,0:T(8,128)S(1)} %fusion.85, f32[8192,256]{1,0:T(8,128)} %bitcast.103, pred[8192]{0:T(1024)(128)(4,1)S(1)} %broadcast_compare_fusion), kind=kOutput, calls=%fused_computation.186 | convolution fusion | flops 1613758336 | bytes 8462848 | tf_op jit(solution)/shard_map/bqhd,khd->bhqk/dot_general | solution.py:127
  300.0 3.5 fusion.6
  303.5 8.0 %fusion.38 = f32[128,128]{0,1:T(8,128)S(1)} fusion(f32[1,8192,1,128]{3,1,2,0:T(8,128)S(1)} %get-tuple-element.19, f32[8192]{0:T(1024)S(1)} %convert_reduce_fusion, f32[128]{0:T(128)S(1)} %broadcast_maximum_fusion, f32[8192,256]{1,0:T(8,128)S(1)} %bitcast.104, f32[128]{0:T(128)S(1)} %fusion.6), kind=kOutput, calls=%fused_computation.40 | convolution fusion | flops 1612726272 | bytes 8487936 | tf_op jit(solution)/shard_map/bhqk,khd->bhqd/dot_general | solution.py:134
  312.0 1.1 broadcast_in_dim.21
  313.1 3.5 all-to-all-start.2
  316.8 5.2 %fusion.97 = f32[2048,128]{1,0:T(8,128)S(1)} fusion(f32[2048,512]{1,0:T(8,128)} %param.21, f32[512,128]{1,0:T(8,128)S(1)} %copy-done.13), kind=kOutput, calls=%fused_computation.191 | convolution fusion | flops 1610612736 | bytes 5505024 | tf_op jit(solution)/shard_map/dot_general | solution.py:38
  322.0 5.3 %all-to-all-done.2 = f32[4,128,512]{2,1,0:T(8,128)S(1)} async-done(((f32[4,128,512]{2,1,0:T(8,128)}), f32[4,128,512]{2,1,0:T(8,128)S(1)}, u32[]{:S(2)}, u32[]{:S(2)}) %all-to-all-start.2) | async-done | bytes 1048608 | tf_op jit(solution)/shard_map/all_to_all | solution.py:14
  328.2 8.2 %collective-permute-start = (f32[128,128]{1,0:T(8,128)S(1)}, f32[128,128]{1,0:T(8,128)S(1)}, u32[]{:S(2)}, u32[]{:S(2)}) collective-permute-start(f32[128,128]{1,0:T(8,128)S(1)} %fusion.46), channel_id=1, source_target_pairs={{0,1},{1,2},{2,3},{3,4},{4,5},{5,6},{6,7},{7,8},{8,9},{9,10},{10,1... | collective-permute-start | bytes 196616 | tf_op jit(solution)/shard_map/ppermute | solution.py:31
  336.5 21.1 %gather_fusion.3 = f32[6144,128]{1,0:T(8,128)} fusion(f32[2048,128]{1,0:T(8,128)S(1)} %fusion.97, s32[6144]{0:T(1024)S(1)} %get-tuple-element.21), kind=kCustom, calls=%fused_computation.3 | custom fusion | bytes 6316032 | tf_op jit(solution)/shard_map/gather | solution.py:53
  357.6 21.1 %gather_fusion.2 = f32[6144,128]{1,0:T(8,128)} fusion(f32[384,128]{1,0:T(8,128)S(1)} %pad_maximum_fusion, s32[6144]{0:T(1024)S(1)} %get-tuple-element.20), kind=kCustom, calls=%fused_computation.2 | custom fusion | bytes 6316032 | tf_op jit(solution)/shard_map/gather | solution.py:53
  378.7 3.2 add.222
  381.8 3.0 fusion.9
  384.8 2.9 fusion.7
  388.1 4.9 %fusion.98 = f32[2048,512]{1,0:T(8,128)} fusion(f32[2048,128]{1,0:T(8,128)S(1)} %bitcast.105, f32[128,512]{1,0:T(8,128)S(1)} %copy-done.14), kind=kOutput, calls=%fused_computation.192 | convolution fusion | flops 1610612736 | bytes 5505024 | tf_op jit(solution)/shard_map/dot_general | solution.py:38
  393.1 46.9 %reduce-scatter.2.cloned.1.call-done = f32[2048,128]{1,0:T(8,128)} async-done(((f32[2048,512]{1,0:T(8,128)}), f32[2048,128]{1,0:T(8,128)}) %reduce-scatter.2.cloned.1.call-update) | async-done | bytes 1048592 | tf_op jit(solution)/shard_map/reduce_scatter | solution.py:153
  440.0 2.6 dynamic-slice_add_fusion
  (140 shorter events, 6.1 us)
Async XLA Ops:
  6.5 95.2 %copy-start = (f32[512,512]{1,0:T(8,128)S(1)}, f32[512,512]{1,0:T(8,128)}, u32[]{:S(2)}) copy-start(f32[512,512]{1,0:T(8,128)} %param.31) | copy-start | bytes 3145732
  14.3 14.2 %copy-start.5 = (f32[128,512]{1,0:T(8,128)S(1)}, f32[128,512]{1,0:T(8,128)}, u32[]{:S(2)}) copy-start(f32[128,512]{1,0:T(8,128)} %param.22) | copy-start | bytes 786436
  14.3 14.2 %copy-start.6 = (f32[512,128]{1,0:T(8,128)S(1)}, f32[512,128]{1,0:T(8,128)}, u32[]{:S(2)}) copy-start(f32[512,128]{1,0:T(8,128)} %param.24) | copy-start | bytes 786436
  28.9 14.2 %copy-start.3 = (f32[4096,128]{1,0:T(8,128)S(1)}, f32[4096,128]{1,0:T(8,128)}, u32[]{:S(2)}) copy-start(f32[4096,128]{1,0:T(8,128)} %gather_fusion) | copy-start | bytes 6291460
  43.1 3.8 copy-start.18
  43.1 5.8 %copy-start.7 = (f32[128,512]{1,0:T(8,128)S(1)}, f32[128,512]{1,0:T(8,128)}, u32[]{:S(2)}) copy-start(f32[128,512]{1,0:T(8,128)} %param.25) | copy-start | bytes 786436
  44.9 23.8 %copy-start.8 = (f32[512,128]{1,0:T(8,128)S(1)}, f32[512,128]{1,0:T(8,128)}, u32[]{:S(2)}) copy-start(f32[512,128]{1,0:T(8,128)} %param.28) | copy-start | bytes 786436
  44.9 23.8 %copy-start.16 = (f32[512]{0:T(512)S(1)}, f32[512]{0:T(512)}, u32[]{:S(2)}) copy-start(f32[512]{0:T(512)} %param.26) | copy-start | bytes 6148
  44.9 24.5 %copy-start.9 = (f32[512,128]{1,0:T(8,128)S(1)}, f32[512,128]{1,0:T(8,128)}, u32[]{:S(2)}) copy-start(f32[512,128]{1,0:T(8,128)} %param.29) | copy-start | bytes 786436
  75.7 25.2 %copy-start.17 = (s32[64,16]{0,1:T(8,128)S(1)}, s32[64,16]{0,1:T(8,128)}, u32[]{:S(2)}) copy-start(s32[64,16]{0,1:T(8,128)} %param.37) | copy-start | bytes 12292
  75.7 25.6 %copy-start.10 = (f32[512,128]{1,0:T(8,128)S(1)}, f32[512,128]{1,0:T(8,128)}, u32[]{:S(2)}) copy-start(f32[512,128]{1,0:T(8,128)} %param.27) | copy-start | bytes 786436
  75.7 26.8 %copy-start.4 = (f32[512,512]{1,0:T(8,128)S(1)}, f32[512,512]{1,0:T(8,128)}, u32[]{:S(2)}) copy-start(f32[512,512]{1,0:T(8,128)} %param.32) | copy-start | bytes 3145732
  75.7 207.5 %all-to-all-start.1 = ((f32[64,128,256]{1,2,0:T(8,128)}), f32[64,128,256]{1,2,0:T(8,128)}, u32[]{:S(2)}, u32[]{:S(2)}) async-start(f32[64,128,256]{1,2,0:T(8,128)} %copy_bitcast_fusion), calls=%async_computation.1 | async-start | bytes 16777216 | tf_op jit(solution)/shard_map/all_to_all | solution.py:118
  292.2 11.3 %copy-start.2 = (f32[64,128,256]{2,1,0:T(8,128)S(1)}, f32[64,128,256]{2,1,0:T(8,128)}, u32[]{:S(2)}) copy-start(f32[64,128,256]{2,1,0:T(8,128)} %copy.41) | copy-start | bytes 25165828
  299.9 11.6 %copy-start.11 = (f32[128,512]{1,0:T(8,128)S(1)}, f32[128,512]{1,0:T(8,128)}, u32[]{:S(2)}) copy-start(f32[128,512]{1,0:T(8,128)} %param.30) | copy-start | bytes 786436
  300.0 16.7 %copy-start.20 = (s32[48,2]{0,1:T(2,128)S(1)}, s32[48,2]{0,1:T(2,128)}, u32[]{:S(2)}) copy-start(s32[48,2]{0,1:T(2,128)} %param.40) | copy-start | bytes 1156
  300.0 16.8 %copy-start.15 = (s32[48,2,128]{2,1,0:T(2,128)S(1)}, s32[48,2,128]{2,1,0:T(2,128)}, u32[]{:S(2)}) copy-start(s32[48,2,128]{2,1,0:T(2,128)} %param.41) | copy-start | bytes 147460
  300.0 16.8 %copy-start.13 = (f32[512,128]{1,0:T(8,128)S(1)}, f32[512,128]{1,0:T(8,128)}, u32[]{:S(2)}) copy-start(f32[512,128]{1,0:T(8,128)} %param.34) | copy-start | bytes 786436
  303.5 24.2 %copy-start.12 = (f32[512,128]{1,0:T(8,128)S(1)}, f32[512,128]{1,0:T(8,128)}, u32[]{:S(2)}) copy-start(f32[512,128]{1,0:T(8,128)} %param.35) | copy-start | bytes 786436
  303.5 24.2 %copy-start.19 = (f32[512]{0:T(512)S(1)}, f32[512]{0:T(512)}, u32[]{:S(2)}) copy-start(f32[512]{0:T(512)} %param.33) | copy-start | bytes 6148
  313.1 14.2 %all-to-all-start.2 = ((f32[4,128,512]{2,1,0:T(8,128)}), f32[4,128,512]{2,1,0:T(8,128)S(1)}, u32[]{:S(2)}, u32[]{:S(2)}) async-start(f32[4,128,512]{2,1,0:T(8,128)} %broadcast_in_dim.21), calls=%async_computation.2 | async-start | bytes 2097152 | tf_op jit(solution)/shard_map/all_to_all | solution.py:14
  316.6 123.3 %reduce-scatter.2.cloned.1.call-start = ((), (), s32[]{:S(2)}) async-start(), calls=%async_computation.4 | async-start | bytes 5242880 | tf_op jit(solution)/shard_map/reduce_scatter | solution.py:153
  328.2 29.4 %collective-permute-start = (f32[128,128]{1,0:T(8,128)S(1)}, f32[128,128]{1,0:T(8,128)S(1)}, u32[]{:S(2)}, u32[]{:S(2)}) collective-permute-start(f32[128,128]{1,0:T(8,128)S(1)} %fusion.46), channel_id=1, source_target_pairs={{0,1},{1,2},{2,3},{3,4},{4,5},{5,6},{6,7},{7,8},{8,9},{9,10},{10,1... | collective-permute-start | bytes 196616 | tf_op jit(solution)/shard_map/ppermute | solution.py:31
  336.4 21.2 %collective-permute-start.1 = (f32[128,128]{1,0:T(8,128)S(1)}, f32[128,128]{1,0:T(8,128)S(1)}, u32[]{:S(2)}, u32[]{:S(2)}) collective-permute-start(f32[128,128]{1,0:T(8,128)S(1)} %fusion.46), channel_id=1, source_target_pairs={{1,0},{2,1},{3,2},{4,3},{5,4},{6,5},{7,6},{8,7},{9,8},{10,9},{11,1... | collective-permute-start | bytes 196616 | tf_op jit(solution)/shard_map/ppermute | solution.py:32
  381.8 6.3 %copy-start.14 = (f32[128,512]{1,0:T(8,128)S(1)}, f32[128,512]{1,0:T(8,128)}, u32[]{:S(2)}) copy-start(f32[128,512]{1,0:T(8,128)} %param.36) | copy-start | bytes 786436
  384.8 57.8 %copy-start.1 = (f32[512,512]{1,0:T(8,128)S(1)}, f32[512,512]{1,0:T(8,128)}, u32[]{:S(2)}) copy-start(f32[512,512]{1,0:T(8,128)} %param.31) | copy-start | bytes 3145732
Sparse Core Ops, SparseCore 0:
  393.2 46.7 reduce-scatter.1
